TPU v7x, 32 devices: a whole 2x2x4 slice. The times are simulated.
32 devices in a mesh: seq: 8 (over z, x), head: 4 (over y, core).
Axes of the slice: x: 2, y: 2, z: 4, core: 2. Of those that a mesh axis runs over, the one named last changes fastest.
Arguments:
- queries: bfloat16 [4096, 64, 128], P('seq', 'head'), may hold values from -41 to 41
- keys: bfloat16 [4096, 64, 128], P('seq', 'head'), may hold values from -6 to 6
- values: bfloat16 [4096, 64, 128], P('seq', 'head'), may hold values from -6 to 6
- cotangent: bfloat16 [4096, 64, 128], P('seq', 'head'), may hold values from -6 to 6
Outputs:
- normed_out: bfloat16 [4096, 64, 128], P('seq', 'head')
- grad_queries: bfloat16 [4096, 64, 128], P('seq', 'head')
- grad_keys: bfloat16 [4096, 64, 128], P('seq', 'head')
- grad_values: bfloat16 [4096, 64, 128], P('seq', 'head')
All inputs are finite; a program needn't handle non-finite values.
Results may differ from a plain program's by a relative error of at most 0.0058.
Values sent between devices are 32-bit elements; how exact they have to be, the bound alone decides.
A program may use at most 128 MiB of HBM per device.

v0:
```python
import jax
import jax.numpy as jnp
from jax import lax
from jax.sharding import PartitionSpec as P

HEADS = 64
BLK = 512


EPSILON = 1e-06


def prefix(value, axis, join, neutral, backward):
    count, mine = (lax.axis_size(axis), lax.axis_index(axis))
    pieces = lax.all_gather(value, axis)
    if backward:
        pieces = pieces[::-1]
        mine = count - 1 - mine
    so_far = jnp.full_like(value, 0) + jnp.asarray(neutral, value.dtype)

    def hop(position, so_far):
        longer = join(so_far, pieces[position])
        return jnp.where(position < mine, longer, so_far)

    return lax.fori_loop(0, count - 1, hop, so_far)


def combine_sum(earlier, later):
    return earlier + later


def local(queries, keys, values, cotangent):
    tok_rows, heads_here, head_dim = queries.shape
    block_count = tok_rows // BLK
    shape4 = (block_count, BLK, heads_here, head_dim)
    q_blocks = queries.reshape(shape4)
    k_blocks = keys.reshape(shape4)
    v_blocks = values.reshape(shape4)
    c_blocks = cotangent.reshape(shape4)
    kv_state = jnp.einsum("nthi,nthj->nhij", k_blocks, v_blocks, preferred_element_type=jnp.float32)
    zero_state = jnp.zeros((1, heads_here, head_dim, head_dim), jnp.float32)
    local_prefix = jnp.concatenate([zero_state, jnp.cumsum(kv_state, axis=0)[:-1]], axis=0)
    own_total = jnp.sum(kv_state, axis=0)
    causal = (jnp.arange(BLK)[:, None] >= jnp.arange(BLK)[None, :])[None, None]
    scores = jnp.einsum("nthd,nshd->nhts", q_blocks, k_blocks, preferred_element_type=jnp.float32)
    weights = jnp.where(causal, scores, 0.0).astype(jnp.bfloat16)
    local_out = jnp.einsum("nhts,nshd->nthd", weights, v_blocks, preferred_element_type=jnp.float32)
    carried = prefix(own_total, "seq", combine_sum, jnp.zeros_like(own_total), False)
    state_low = (carried[None] + local_prefix).astype(jnp.bfloat16)
    raw_out = local_out + jnp.einsum(
        "nthi,nhij->nthj", q_blocks, state_low, preferred_element_type=jnp.float32
    )
    width = HEADS * head_dim
    cot_float = c_blocks.astype(jnp.float32)
    sum_squares = jnp.sum(raw_out * raw_out, axis=(2, 3))
    total_sq = lax.psum(sum_squares, "head")
    inv_rms = lax.rsqrt(total_sq / width + EPSILON)[..., None, None]
    normed = raw_out * inv_rms
    inner = lax.psum(jnp.sum(cot_float * normed, axis=(2, 3)), "head")
    slope = (inner / width)[..., None, None]
    normed_out = normed.astype(jnp.bfloat16)
    grad_raw = (inv_rms * (cot_float - normed * slope)).astype(jnp.bfloat16)
    qg_state = jnp.einsum("nthi,nthj->nhij", q_blocks, grad_raw, preferred_element_type=jnp.float32)
    reverse_sum = jnp.cumsum(qg_state[::-1], axis=0)[::-1]
    local_suffix = jnp.concatenate([reverse_sum[1:], zero_state], axis=0)
    later_total = prefix(
        jnp.sum(qg_state, axis=0), "seq", combine_sum, jnp.zeros_like(own_total), True
    )
    suffix_low = (later_total[None] + local_suffix).astype(jnp.bfloat16)
    gscores = jnp.einsum("nthj,nshj->nhts", grad_raw, v_blocks, preferred_element_type=jnp.float32)
    gweights = jnp.where(causal, gscores, 0.0).astype(jnp.bfloat16)
    grad_q = jnp.einsum("nhts,nshi->nthi", gweights, k_blocks, preferred_element_type=jnp.float32)
    grad_q = grad_q + jnp.einsum(
        "nthj,nhij->nthi", grad_raw, state_low, preferred_element_type=jnp.float32
    )
    grad_k = jnp.einsum("nhts,nthi->nshi", gweights, q_blocks, preferred_element_type=jnp.float32)
    grad_k = grad_k + jnp.einsum(
        "nshj,nhij->nshi", v_blocks, suffix_low, preferred_element_type=jnp.float32
    )
    grad_v = jnp.einsum("nhts,nthj->nshj", weights, grad_raw, preferred_element_type=jnp.float32)
    grad_v = grad_v + jnp.einsum(
        "nshi,nhij->nshj", k_blocks, suffix_low, preferred_element_type=jnp.float32
    )
    full = (tok_rows, heads_here, head_dim)
    return (
        normed_out.reshape(full),
        grad_q.astype(jnp.bfloat16).reshape(full),
        grad_k.astype(jnp.bfloat16).reshape(full),
        grad_v.astype(jnp.bfloat16).reshape(full),
    )


def solution(mesh):
    return jax.shard_map(
        local,
        mesh=mesh,
        in_specs=(
            P("seq", "head", None),
            P("seq", "head", None),
            P("seq", "head", None),
            P("seq", "head", None),
        ),
        out_specs=(
            P("seq", "head", None),
            P("seq", "head", None),
            P("seq", "head", None),
            P("seq", "head", None),
        ),
        check_vma=False,
    )
```

profile of v0, /device:TPU:0, one launch (start us, length us, event | category | flops | bytes accessed | tf_op | source)
XLA Modules:
  0.0 358.5 jit_solution(8820109877633874767)
XLA Ops:
  8.8 4.5 %fusion.15 = f32[16,128,128]{2,1,0:T(8,128)} fusion(bf16[512,16,128]{2,1,0:T(8,128)(2,1)S(1)} %copy-done, bf16[512,16,128]{2,1,0:T(8,128)(2,1)} %param.9), kind=kOutput, calls=%fused_computation.30 | convolution fusion | flops 268435456 | bytes 5242880 | tf_op jit(solution)/shard_map/nthi,nthj->nhij/dot_general | solution.py:40
  13.4 4.3 %copy.40 = bf16[512,16,128]{0,2,1:T(8,128)(2,1)} copy(bf16[512,16,128]{2,1,0:T(8,128)(2,1)} %param.11) | data formatting | bytes 4194304 | tf_op args[3]
  17.7 9.0 %select_convert_fusion.1 = bf16[16,512,512]{2,1,0:T(8,128)(2,1)} fusion(pred[512,512]{1,0:T(8,128)(4,1)S(1)} %iota_compare_fusion, bf16[512,16,128]{2,1,0:T(8,128)(2,1)} %param.9, bf16[512,16,128]{2,1,0:T(8,128)(2,1)} %param.8), kind=kOutput, calls=%fused_computation.3 | convolution fusion | flops 1082130432 | bytes 12845056 | tf_op jit(solution)/shard_map/nthd,nshd->nhts/dot_general | solution.py:45
  26.7 114.3 %all-gather.5.cloned.1.call-done = f32[128,128,128]{2,1,0:T(8,128)} async-done(((f32[16,128,128]{2,1,0:T(8,128)}), f32[128,128,128]{2,1,0:T(8,128)}) %all-gather.5.cloned.1.call-update) | async-done | bytes 8388624 | tf_op jit(solution)/shard_map/all_gather | solution.py:15
  141.1 11.3 %while.28 = (s32[]{:T(128)}, f32[16,128,128]{2,1,0:T(8,128)S(1)}, s32[]{:T(128)}, f32[8,16,128,128]{3,2,1,0:T(8,128)}, s32[]{:T(128)}, /*index=5*/s32[]{:T(128)}) while((s32[]{:T(128)}, f32[16,128,128]{2,1,0:T(8,128)S(1)}, s32[]{:T(128)}, f32[8,16,128,128]{3,2,1,0:T(8,128)}, s32[]{:T(128)}, /*index=5*/s32[]{:T(128)}) %tuple.76), condition=%wide.region_1.2_spmd.clone, body=%wide.region_0.0_spmd.clone.sunk | while | flops 786436 | bytes 3145829 | solution.py:25
  152.4 3.2 fusion.23
  155.6 8.2 %fusion.5 = (f32[512]{0:T(512)S(1)}, f32[16,128,512]{2,1,0:T(8,128)}) fusion(f32[16,128,512]{2,1,0:T(8,128)S(1)} %fusion.23, bf16[16,512,512]{2,1,0:T(8,128)(2,1)} %select_convert_fusion.1, bf16[512,16,128]{2,1,0:T(8,128)(2,1)S(1)} %copy-done), kind=kOutput, calls=%fused_computation.17 | convolution fusion | flops 1076887040 | bytes 18876416 | tf_op jit(solution)/shard_map/nhts,nshd->nthd/dot_general | solution.py:47
  163.8 6.1 %psum.14 = f32[1,512]{1,0:T(1,128)S(1)} all-reduce(f32[1,512]{1,0:T(1,128)S(1)} %bitcast.96), channel_id=1, replica_groups=mesh['seq'=8,'head'=4] {'head'}, use_global_device_ids=true, to_apply=%region_3.4 | all-reduce | flops 512 | bytes 4096 | tf_op jit(solution)/shard_map/psum | solution.py:56
  170.0 3.5 fusion
  173.5 6.3 %psum.15 = f32[1,512]{1,0:T(1,128)S(1)} all-reduce(f32[1,512]{1,0:T(1,128)S(1)} %bitcast.98), channel_id=1, replica_groups=mesh['seq'=8,'head'=4] {'head'}, use_global_device_ids=true, to_apply=%region_5.6 | all-reduce | flops 512 | bytes 4096 | tf_op jit(solution)/shard_map/psum | solution.py:59
  179.8 3.8 %fusion.7 = bf16[512,16,128]{0,2,1:T(8,128)(2,1)S(1)} fusion(f32[16,128,512]{2,1,0:T(8,128)} %get-tuple-element.219, bf16[512,16,128]{0,2,1:T(8,128)(2,1)} %copy.40, f32[512]{0:T(512)S(1)} %bitcast.97, f32[512]{0:T(512)S(1)} %bitcast.94), kind=kLoop, calls=%fused_computation.21 | loop fusion | flops 6291456 | bytes 8392704 | tf_op jit(solution)/shard_map/reshape.31
  187.5 4.1 %fusion.6 = bf16[512,16,128]{0,2,1:T(8,128)(2,1)} fusion(f32[16,128,512]{2,1,0:T(8,128)} %get-tuple-element.219, f32[512]{0:T(512)S(1)} %bitcast.95), kind=kLoop, calls=%fused_computation.20 | loop fusion | flops 2097152 | bytes 6293504 | tf_op jit(solution)/shard_map/reshape | solution.py:86
  191.6 4.6 %copy.54 = bf16[512,16,128]{2,1,0:T(8,128)(2,1)} copy(bf16[512,16,128]{0,2,1:T(8,128)(2,1)} %fusion.6) | data formatting | bytes 4194304
  196.2 2.8 fusion.28
  199.0 6.3 %select_convert_fusion = bf16[16,512,512]{2,1,0:T(8,128)(2,1)} fusion(bf16[512,16,128]{0,2,1:T(8,128)(2,1)S(1)} %copy-done.3, pred[512,512]{1,0:T(8,128)(4,1)S(1)} %iota_compare_fusion, bf16[512,16,128]{2,1,0:T(8,128)(2,1)S(1)} %copy-done), kind=kOutput, calls=%fused_computation.2 | convolution fusion | flops 1082130432 | bytes 12845056 | tf_op jit(solution)/shard_map/nthj,nshj->nhts/dot_general | solution.py:70
  205.3 6.2 %fusion.8 = bf16[512,16,128]{2,0,1:T(8,128)(2,1)S(1)} fusion(f32[16,128,512]{1,2,0:T(8,128)S(1)} %fusion.28, bf16[16,512,512]{2,1,0:T(8,128)(2,1)} %select_convert_fusion, bf16[512,16,128]{2,1,0:T(8,128)(2,1)S(1)} %copy-done.6), kind=kOutput, calls=%fused_computation.22 | convolution fusion | flops 1075838976 | bytes 16777216 | tf_op jit(solution)/shard_map/nhts,nshi->nthi/dot_general | solution.py:72
  214.2 3.2 fusion.31
  217.4 92.8 %all-gather.7.cloned.1.call-done = f32[128,128,128]{2,1,0:T(8,128)} async-done(((f32[16,128,128]{2,1,0:T(8,128)}), f32[128,128,128]{2,1,0:T(8,128)}) %all-gather.7.cloned.1.call-update) | async-done | bytes 8388624 | tf_op jit(solution)/shard_map/all_gather | solution.py:15
  310.2 7.7 %rev.3 = f32[8,16,128,128]{3,2,1,0:T(8,128)} reverse(f32[8,16,128,128]{3,2,1,0:T(8,128)} %bitcast.91), dimensions={0} | reverse | bytes 16777216 | tf_op jit(solution)/shard_map/rev | solution.py:17
  317.9 11.3 %while.29 = (s32[]{:T(128)}, f32[16,128,128]{2,1,0:T(8,128)S(1)}, s32[]{:T(128)}, f32[8,16,128,128]{3,2,1,0:T(8,128)}, s32[]{:T(128)}, /*index=5*/s32[]{:T(128)}) while((s32[]{:T(128)}, f32[16,128,128]{2,1,0:T(8,128)S(1)}, s32[]{:T(128)}, f32[8,16,128,128]{3,2,1,0:T(8,128)}, s32[]{:T(128)}, /*index=5*/s32[]{:T(128)}) %tuple.69), condition=%wide.region_7.8_spmd.clone, body=%wide.region_6.7_spmd.clone.sunk | while | flops 786436 | bytes 3145829 | solution.py:25
  329.2 2.9 fusion.12
  333.6 2.7 fusion.10
  336.3 4.5 %copy.57 = bf16[512,16,128]{2,1,0:T(8,128)(2,1)} copy(bf16[512,16,128]{0,2,1:T(8,128)(2,1)} %fusion.10) | data formatting | bytes 4194304
  340.8 8.1 %fusion.9 = bf16[512,16,128]{2,0,1:T(8,128)(2,1)S(1)} fusion(f32[16,128,512]{1,2,0:T(8,128)} %fusion.12, bf16[16,512,512]{2,1,0:T(8,128)(2,1)} %select_convert_fusion, bf16[512,16,128]{2,1,0:T(8,128)(2,1)} %param.8), kind=kOutput, calls=%fused_computation.23 | convolution fusion | flops 1075838976 | bytes 16777216 | tf_op jit(solution)/shard_map/nhts,nthi->nshi/dot_general | solution.py:76
  (48 shorter events, 34.7 us)
Async XLA Ops:
  7.2 1.6 copy-start
  7.2 133.9 %all-gather.5.cloned.1.call-start = ((), (), s32[]{:S(2)}) async-start(), calls=%async_computation | async-start | bytes 9437184 | tf_op jit(solution)/shard_map/all_gather | solution.py:15
  13.3 296.9 %all-gather.7.cloned.1.call-start = ((), (), s32[]{:S(2)}) async-start(), calls=%async_computation.1 | async-start | bytes 9437184 | tf_op jit(solution)/shard_map/all_gather | solution.py:15
  152.4 3.2 copy-start.1
  179.8 5.2 %copy-start.5 = (bf16[512,16,128]{2,1,0:T(8,128)(2,1)S(1)}, bf16[512,16,128]{2,1,0:T(8,128)(2,1)}, u32[]{:S(2)}) copy-start(bf16[512,16,128]{2,1,0:T(8,128)(2,1)} %param.8) | copy-start | bytes 6291460
  183.6 1.3 copy-start.2
  196.2 2.8 copy-start.3
  199.0 6.3 %copy-start.6 = (bf16[512,16,128]{2,1,0:T(8,128)(2,1)S(1)}, bf16[512,16,128]{2,1,0:T(8,128)(2,1)}, u32[]{:S(2)}) copy-start(bf16[512,16,128]{2,1,0:T(8,128)(2,1)} %param.9) | copy-start | bytes 6291460
  199.0 15.1 %slice-start = ((s8[8388608]{0:T(1024)(128)(4,1)}), s8[4194304]{0:T(1024)(128)(4,1)S(1)}, s32[]{:S(2)}) async-start(s8[8388608]{0:T(1024)(128)(4,1)} %bitcast.89), calls=%async_computation.2 | async-start | bytes 8388608
  205.3 8.9 %slice-start.1 = ((s8[8388608]{0:T(1024)(128)(4,1)}), s8[4194304]{0:T(1024)(128)(4,1)S(1)}, s32[]{:S(2)}) async-start(s8[8388608]{0:T(1024)(128)(4,1)} %bitcast.89), calls=%async_computation.3 | async-start | bytes 8388608
  329.2 3.4 copy-start.4
  329.2 4.4 %copy-start.7 = (bf16[512,16,128]{2,1,0:T(8,128)(2,1)S(1)}, bf16[512,16,128]{2,1,0:T(8,128)(2,1)}, u32[]{:S(2)}) copy-start(bf16[512,16,128]{2,1,0:T(8,128)(2,1)} %param.9) | copy-start | bytes 6291460
Sparse Core Ops, SparseCore 0:
  13.4 127.6 all-gather.4
  187.6 122.5 all-gather.6
where the time goes:
time: 360 us; the launch traced here: 358 us
  waiting for transfers between devices  207 us (58%)
  matrix products  58.4 us (16%)
  other arithmetic  33.8 us (9%)
  local copies, waits for them, and re-layouts  32.2 us (9%)
  between operations  14.2 us (4%)
  blocking collectives  12.4 us (3%)
    all_gather x2, waiting for transfers between devices, prefix(): pieces = lax.all_gather(value, axis)  207 us
    unnamed x25, local copies, waits for them, and re-layouts  23.1 us
    select_n x14, other arithmetic, hop(): return jnp.where(position < mine, longer, so_far)  22.2 us
    dot_general x1, matrix products, local(): jnp.einsum('nthd,nshd->nhts', q_blocks, k_blocks, preferred_element_type=...  9.01 us
    dot_general x1, matrix products, local(): jnp.einsum('nhts,nshd->nthd', weights, v_blocks, preferred_element_type=j...  8.25 us
    dot_general x1, matrix products, local(): jnp.einsum('nhts,nthi->nshi', gweights, q_blocks, preferred_element_type=...  8.13 us
    rev x1, local copies, waits for them, and re-layouts, prefix(): pieces = pieces[::-1]  7.72 us
  transfers between devices with their start and end apart: 2, of which 2 were waited for; matrix products, arithmetic and copies ran while one was open for 12% of the time, Pallas kernels for 0%

commit v1 on v0

v1 whole, which is shorter than its diff:
```python
import functools

import jax
import jax.numpy as jnp
from jax import lax
from jax.experimental import pallas as pl
from jax.experimental.pallas import tpu as pltpu
from jax.sharding import PartitionSpec as P

EPSILON = 1e-06
CUT = 256
PARTS = 4
F32 = jnp.float32
BF16 = jnp.bfloat16
MESH = pl.DeviceIdType.MESH


def dot(a, b):
    return lax.dot_general(a, b, (((1,), (0,)), ((), ())), preferred_element_type=F32)


def dot_nt(a, b):
    return lax.dot_general(a, b, (((1,), (1,)), ((), ())), preferred_element_type=F32)


def dot_tn(a, b):
    return lax.dot_general(a, b, (((0,), (0,)), ((), ())), preferred_element_type=F32)


def kernel(n, nh, heads, toks, dim,
           q_hbm, k_hbm, v_hbm, c_hbm, no_hbm, gq_hbm, gk_hbm, gv_hbm,
           io, st0, st1, st2, st3, qh, kh, vh, ch, raw, gr,
           own, rs, rp, rx, sp, sx, low, acc, ex_send, ex_recv,
           in_sem, out_sem, rs_s, rs_r, rp_s, rp_r, rx_s, rx_r, ex_s, ex_r):
    half = heads // 2
    pairs = n // 2
    rows = toks * heads
    width = heads * nh * dim
    stages = (st0, st1, st2, st3)
    outs = (no_hbm, gq_hbm, gk_hbm, gv_hbm)
    seq = lax.axis_index("seq")
    me = lax.axis_index("head")
    pair = seq // 2
    side = seq % 2
    partner = seq + 1 - 2 * side
    own_base = side * half
    oth_base = (1 - side) * half

    loads = [
        pltpu.make_async_copy(src, io.at[a], in_sem.at[a])
        for a, src in enumerate((k_hbm, v_hbm, q_hbm, c_hbm))
    ]
    for load in loads:
        load.start()

    barrier = pltpu.get_barrier_semaphore()
    pl.semaphore_signal(barrier, inc=1, device_id={"seq": partner}, device_id_type=MESH)

    @pl.when(pair > 0)
    def _():
        pl.semaphore_signal(barrier, inc=1, device_id={"seq": (seq + n - 2) % n}, device_id_type=MESH)

    @pl.when(pair < pairs - 1)
    def _():
        pl.semaphore_signal(barrier, inc=1, device_id={"seq": (seq + 2) % n}, device_id_type=MESH)

    for d in range(1, nh):
        pl.semaphore_signal(barrier, inc=1, device_id={"head": (me + d) % nh}, device_id_type=MESH)

    def strided(ref, h):
        return ref.at[pl.ds(h, toks, stride=heads), :]

    chunk = rows // 16

    def widen(a):
        def body(j, _):
            at = pl.ds(pl.multiple_of(j * chunk, chunk), chunk)
            stages[a][at, :] = io[a, at, :].astype(F32)
            return 0
        lax.fori_loop(0, 16, body, 0)

    def store_copy(a, j):
        part = rows // PARTS
        at = pl.ds(j * part, part)
        return pltpu.make_async_copy(io.at[a, at], outs[a].at[at], out_sem.at[a, j])

    def narrow(a):
        for j in range(PARTS):
            def body(t, _, j=j):
                at = pl.ds(pl.multiple_of((j * (16 // PARTS) + t) * chunk, chunk), chunk)
                io[a, at, :] = stages[a][at, :].astype(BF16)
                return 0
            lax.fori_loop(0, 16 // PARTS, body, 0)
            store_copy(a, j).start()

    def swap(ph, c):
        return pltpu.make_async_remote_copy(
            src_ref=own.at[ph, oth_base + c], dst_ref=rs.at[ph, c],
            send_sem=rs_s.at[ph, c], recv_sem=rs_r.at[ph, c],
            device_id={"seq": partner}, device_id_type=MESH)

    def chain(ph, c):
        nxt = (seq + 2) % n if ph == 0 else (seq + n - 2) % n
        return pltpu.make_async_remote_copy(
            src_ref=sp.at[ph, c], dst_ref=rp.at[ph, c],
            send_sem=rp_s.at[ph, c], recv_sem=rp_r.at[ph, c],
            device_id={"seq": nxt}, device_id_type=MESH)

    def hand(ph, c):
        return pltpu.make_async_remote_copy(
            src_ref=sx.at[ph, c], dst_ref=rx.at[ph, c],
            send_sem=rx_s.at[ph, c], recv_sem=rx_r.at[ph, c],
            device_id={"seq": partner}, device_id_type=MESH)

    def place(ph):
        return pair if ph == 0 else pairs - 1 - pair

    def relay(ph, c):
        at = place(ph)
        later = (side == 1) if ph == 0 else (side == 0)
        swap(ph, c).wait_recv()
        mine = own[ph, own_base + c]
        theirs = rs[ph, c]

        @pl.when(at > 0)
        def _():
            chain(ph, c).wait_recv()

        so_far = rp[ph, c]

        @pl.when(at < pairs - 1)
        def _():
            sp[ph, c] = so_far + (mine + theirs)
            chain(ph, c).start()

        sx[ph, c] = so_far + jnp.where(later, 0.0, mine)
        hand(ph, c).start()
        low[ph, own_base + c] = (so_far + jnp.where(later, theirs, 0.0)).astype(BF16)

    def take(ph, c):
        hand(ph, c).wait_recv()
        low[ph, oth_base + c] = rx[ph, c].astype(BF16)

    def scan(ph, unit, finish, after_units):
        at = place(ph)

        def done_units(c):
            return jnp.where(c < 0, 0, jnp.minimum(heads, 2 * (c + 1) + 5 * at))

        def done_takes(c):
            lag = 2 + 2 * (pairs - 1 - at)
            return jnp.clip(c + 1 - lag, 0, half)

        def slot(c, _):
            def one(u, _):
                unit(jnp.where(u % 2 == 0, own_base, oth_base) + u // 2)
                return 0
            lax.fori_loop(done_units(c - 1), done_units(c), one, 0)
            if after_units is not None:
                @pl.when((done_units(c) == heads) & (done_units(c - 1) < heads))
                def _():
                    after_units()
            relay(ph, c)
            finish(own_base + c)
            lax.fori_loop(done_takes(c - 1), done_takes(c), take_one, 0)
            return 0

        def take_one(c, _):
            take(ph, c)
            finish(oth_base + c)
            return 0

        lax.fori_loop(0, half, slot, 0)
        lax.fori_loop(done_takes(half - 1), half, take_one, 0)

    for ph in range(2):
        @pl.when(place(ph) == 0)
        def _():
            rp[ph] = jnp.zeros(rp.shape[1:], F32)

    acc[...] = jnp.zeros(acc.shape, F32)
    loads[0].wait()
    widen(0)
    loads[1].wait()
    widen(1)
    pl.semaphore_wait(
        barrier, nh + jnp.where(pair > 0, 1, 0) + jnp.where(pair < pairs - 1, 1, 0))

    def kv_state(h):
        k = strided(st0, h)[...].astype(BF16)
        v = strided(st1, h)[...].astype(BF16)
        kh[h] = k
        vh[h] = v
        own[0, h] = dot_tn(k, v)

    def kv_other(c, _):
        kv_state(oth_base + c)
        swap(0, c).start()
        return 0

    def kv_own(c, _):
        kv_state(own_base + c)
        return 0

    lax.fori_loop(0, half, kv_other, 0)
    lax.fori_loop(0, half, kv_own, 0)
    loads[2].wait()
    widen(2)
    loads[3].wait()
    widen(3)

    def split_qc(h, _):
        qh[h] = strided(st2, h)[...].astype(BF16)
        ch[h] = strided(st3, h)[...].astype(BF16)
        return 0

    lax.fori_loop(0, heads, split_qc, 0)

    rest = toks - CUT

    def below(shape, shift):
        return (lax.broadcasted_iota(jnp.int32, shape, 1)
                <= lax.broadcasted_iota(jnp.int32, shape, 0) + shift)

    def above(shape):
        return (lax.broadcasted_iota(jnp.int32, shape, 1)
                >= lax.broadcasted_iota(jnp.int32, shape, 0))

    def keep(mask, x):
        return jnp.where(mask, x, 0.0).astype(BF16)

    def lower(a, b, c):
        w0 = keep(below((CUT, CUT), 0), dot_nt(a[:CUT], b[:CUT]))
        w1 = keep(below((rest, toks), CUT), dot_nt(a[CUT:], b))
        return dot(w0, c[:CUT]), dot(w1, c)

    def upper(a, b, c):
        w0 = keep(above((CUT, toks)), dot_nt(a[:CUT], b))
        w1 = keep(above((rest, rest)), dot_nt(a[CUT:], b[CUT:]))
        return dot(w0, c), dot(w1, c[CUT:])

    def local_out(h):
        first, second = lower(qh[h], kh[h], vh[h])
        raw[h, :CUT] = first
        raw[h, CUT:] = second

    def finish_out(h):
        r = raw[h] + dot(qh[h], low[0, h])
        raw[h] = r
        acc[0] += r * r
        acc[1] += ch[h].astype(F32) * r

    scan(0, local_out, finish_out, None)

    sq = jnp.sum(acc[0].T, axis=0, keepdims=True)
    inner = jnp.sum(acc[1].T, axis=0, keepdims=True)
    row = lax.broadcasted_iota(jnp.int32, (8, toks), 0)
    ex_send[...] = jnp.where(row < 4, jnp.broadcast_to(sq, (8, toks)), jnp.broadcast_to(inner, (8, toks)))
    peers = [
        pltpu.make_async_remote_copy(
            src_ref=ex_send, dst_ref=ex_recv.at[d - 1],
            send_sem=ex_s.at[d - 1], recv_sem=ex_r.at[d - 1],
            device_id={"head": (me + d) % nh}, device_id_type=MESH)
        for d in range(1, nh)
    ]
    for peer in peers:
        peer.start()
    total = ex_send[...]
    for d, peer in enumerate(peers):
        peer.wait_recv()
        total = total + ex_recv[d]
    inv = lax.rsqrt(total[0:1] / width + EPSILON)
    slope = inv * (total[4:5] / width)
    acc[0] = jnp.broadcast_to(inv, (dim, toks)).T
    acc[1] = jnp.broadcast_to(inv * slope, (dim, toks)).T

    def qg_state(h):
        g = (acc[0] * (ch[h].astype(F32) - raw[h] * acc[1])).astype(BF16)
        gr[h] = g
        own[1, h] = dot_tn(qh[h], g)

    def qg_other(c, _):
        qg_state(oth_base + c)
        swap(1, c).start()
        return 0

    def qg_own(c, _):
        qg_state(own_base + c)
        return 0

    lax.fori_loop(0, half, qg_other, 0)
    lax.fori_loop(0, half, qg_own, 0)

    def local_grads(h):
        q, k, v, g = qh[h], kh[h], vh[h], gr[h]
        strided(st0, h)[...] = raw[h] * acc[0]
        first, second = lower(g, v, k)
        strided(st1, h)[...] = jnp.concatenate([first, second], axis=0) + dot_nt(g, low[0, h])
        first, second = upper(v, g, q)
        strided(st2, h)[...] = jnp.concatenate([first, second], axis=0)
        first, second = upper(k, q, g)
        strided(st3, h)[...] = jnp.concatenate([first, second], axis=0)

    def early_outs():
        narrow(0)
        narrow(1)

    def finish_grads(h):
        strided(st2, h)[...] = strided(st2, h)[...] + dot_nt(vh[h], low[1, h])
        strided(st3, h)[...] = strided(st3, h)[...] + dot(kh[h], low[1, h])

    scan(1, local_grads, finish_grads, early_outs)
    narrow(2)
    narrow(3)

    for peer in peers:
        peer.wait_send()
    for ph in range(2):
        def drain(c, _, ph=ph):
            swap(ph, c).wait_send()
            hand(ph, c).wait_send()

            @pl.when(place(ph) < pairs - 1)
            def _():
                chain(ph, c).wait_send()
            return 0
        lax.fori_loop(0, half, drain, 0)
    for a in range(4):
        for j in range(PARTS):
            store_copy(a, j).wait()


def local(n, nh, queries, keys, values, cotangent):
    toks, heads, dim = queries.shape
    rows = toks * heads
    half = heads // 2
    flat = [x.reshape(rows, dim) for x in (queries, keys, values, cotangent)]
    any_spec = pl.BlockSpec(memory_space=pl.ANY)
    sems = pltpu.SemaphoreType.DMA
    per_head = pltpu.VMEM((heads, toks, dim), BF16)
    part = pltpu.VMEM((2, half, dim, dim), F32)
    outs = pl.pallas_call(
        functools.partial(kernel, n, nh, heads, toks, dim),
        out_shape=[jax.ShapeDtypeStruct((rows, dim), BF16)] * 4,
        in_specs=[any_spec] * 4,
        out_specs=[any_spec] * 4,
        scratch_shapes=[
            pltpu.VMEM((4, rows, dim), BF16),
            *[pltpu.VMEM((rows, dim), F32)] * 4,
            *[per_head] * 4,
            pltpu.VMEM((heads, toks, dim), F32),
            per_head,
            pltpu.VMEM((2, heads, dim, dim), F32),
            *[part] * 5,
            pltpu.VMEM((2, heads, dim, dim), BF16),
            pltpu.VMEM((2, toks, dim), F32),
            pltpu.VMEM((8, toks), F32),
            pltpu.VMEM((nh - 1, 8, toks), F32),
            sems((4,)),
            sems((4, PARTS)),
            *[sems((2, half))] * 6,
            sems((nh - 1,)),
            sems((nh - 1,)),
        ],
        compiler_params=pltpu.CompilerParams(
            collective_id=0, has_side_effects=True, vmem_limit_bytes=60 * 2**20),
        cost_estimate=pl.CostEstimate(
            flops=heads * 10 * toks * toks * dim, bytes_accessed=16 * rows * dim, transcendentals=toks),
    )(*flat)
    return tuple(x.reshape(toks, heads, dim) for x in outs)


def solution(mesh):
    n, nh = mesh.shape["seq"], mesh.shape["head"]
    spec = P("seq", "head", None)
    return jax.shard_map(
        functools.partial(local, n, nh),
        mesh=mesh,
        in_specs=(spec,) * 4,
        out_specs=(spec,) * 4,
        check_vma=False,
    )
```

time: 360 us -> 100 us (0.28)
  waiting for transfers between devices: 207 us -> 0 us
  Pallas kernels: 0 us -> 89.9 us
  matrix products: 58.4 us -> 0 us
  other arithmetic: 33.8 us -> 0 us
  local copies, waits for them, and re-layouts: 32.2 us -> 9.43 us
  between operations: 14.2 us -> 0.65 us
  blocking collectives: 12.4 us -> 0 us
    all_gather x2 -> x0, waiting for transfers between devices: 207 us -> none  [prefix(): pieces = lax.all_gather(value, axis)]
    pallas_call x0 -> x1, Pallas kernels: none -> 89.9 us  [local(): pl.pallas_call(functools.partial(kernel, n, nh, heads, toks, dim), out_sh...]
    dot_general x12 -> x0, matrix products: 58.4 us -> none  [the longest x1 9.01 us: local(): jnp.einsum('nthd,nshd->nhts', q_blocks, k_blocks, preferred_element_type=...]
    select_n x14 -> x0, other arithmetic: 22.2 us -> none  [hop(): return jnp.where(position < mine, longer, so_far)]
    unnamed x25 -> x10, local copies, waits for them, and re-layouts: 23.1 us -> 9.43 us
    psum x2 -> x0, blocking collectives: 12.4 us -> none  [the longest x1 6.28 us: local(): inner = lax.psum(jnp.sum(cot_float * normed, axis=(2, 3)), 'head')]
    rev x1 -> x0, local copies, waits for them, and re-layouts: 7.72 us -> none  [prefix(): pieces = pieces[::-1]]
    reshape x1 -> x0, other arithmetic: 4.12 us -> none  [local(): normed_out.reshape(full)]
  transfers between devices with their start and end apart: 2 -> 0, of which waited for: 2 -> 0; matrix products, arithmetic and copies ran while one was open for 12% -> 0% of each run, Pallas kernels for 0% -> 0%
where the time goes in v1:
time: 100 us
  Pallas kernels  89.9 us (90%)
  local copies, waits for them, and re-layouts  9.43 us (9%)
    pallas_call x1, Pallas kernels, local(): pl.pallas_call(functools.partial(kernel, n, nh, heads, toks, dim), out_sh...  89.9 us
    unnamed x10, local copies, waits for them, and re-layouts  9.43 us

profile of v1, /device:TPU:0, one launch (start us, length us, event | category | flops | bytes accessed | tf_op | source)
XLA Modules:
  0.0 100.0 jit_solution(1401286573252783688)
XLA Ops:
  0.6 89.9 %shard_map.75 = (bf16[8192,128]{1,0:T(8,128)(2,1)}, bf16[8192,128]{1,0:T(8,128)(2,1)}, bf16[8192,128]{1,0:T(8,128)(2,1)}, bf16[8192,128]{1,0:T(8,128)(2,1)}) custom-call(bf16[8192,128]{1,0:T(8,128)(2,1)} %bitcast.12, bf16[8192,128]{1,0:T(8,128)(2,1)} %bitcast.13, bf16[8192,128]{1,0:T(8,128)(2,1)} %bitcast.14, bf16[8192,128]{1,0:T(8,128)(2,1)} %bitcast.15), custom_call_target="tpu_custom_call" | custom-call | flops 5368709120 | bytes 16777216 | tf_op jit(solution)/shard_map/pallas_call | solution.py:342
  90.5 0.0 copy-start.2
  90.6 3.4 %copy.12 = bf16[512,16,128]{2,1,0:T(8,128)(2,1)} copy(bf16[512,16,128]{2,1,0:T(8,128)(2,1)} %bitcast.11) | data formatting | bytes 4194304
  94.0 0.0 copy-done.2
  94.0 0.0 copy-start.1
  94.0 1.3 %copy.13 = bf16[512,16,128]{2,1,0:T(8,128)(2,1)} copy(bf16[512,16,128]{2,1,0:T(8,128)(2,1)S(1)} %bitcast.10) | data formatting | bytes 4194304
  95.3 1.0 %copy-done.1 = bf16[8192,128]{1,0:T(8,128)(2,1)S(1)} copy-done((bf16[8192,128]{1,0:T(8,128)(2,1)S(1)}, bf16[8192,128]{1,0:T(8,128)(2,1)}, u32[]{:S(2)}) %copy-start.1) | copy-done | bytes 2097176
  96.3 0.0 copy-start
  96.3 1.3 %copy.14 = bf16[512,16,128]{2,1,0:T(8,128)(2,1)} copy(bf16[512,16,128]{2,1,0:T(8,128)(2,1)S(1)} %bitcast.9) | data formatting | bytes 4194304
  97.6 1.0 %copy-done = bf16[8192,128]{1,0:T(8,128)(2,1)S(1)} copy-done((bf16[8192,128]{1,0:T(8,128)(2,1)S(1)}, bf16[8192,128]{1,0:T(8,128)(2,1)}, u32[]{:S(2)}) %copy-start) | copy-done | bytes 2097176
  98.7 1.3 %copy.15 = bf16[512,16,128]{2,1,0:T(8,128)(2,1)} copy(bf16[512,16,128]{2,1,0:T(8,128)(2,1)S(1)} %bitcast.8) | data formatting | bytes 4194304
Async XLA Ops:
  90.5 3.4 %copy-start.2 = (bf16[8192,128]{1,0:T(8,128)(2,1)S(1)}, bf16[8192,128]{1,0:T(8,128)(2,1)}, u32[]{:S(2)}) copy-start(bf16[8192,128]{1,0:T(8,128)(2,1)} %get-tuple-element.9) | copy-start | bytes 6291460
  94.0 2.3 %copy-start.1 = (bf16[8192,128]{1,0:T(8,128)(2,1)S(1)}, bf16[8192,128]{1,0:T(8,128)(2,1)}, u32[]{:S(2)}) copy-start(bf16[8192,128]{1,0:T(8,128)(2,1)} %get-tuple-element.10) | copy-start | bytes 6291460
  96.3 2.3 %copy-start = (bf16[8192,128]{1,0:T(8,128)(2,1)S(1)}, bf16[8192,128]{1,0:T(8,128)(2,1)}, u32[]{:S(2)}) copy-start(bf16[8192,128]{1,0:T(8,128)(2,1)} %get-tuple-element.11) | copy-start | bytes 6291460

commit v2 on v1

--- a/solution.py
+++ b/solution.py
@@ -28,16 +28,14 @@
 
 
 def kernel(n, nh, heads, toks, dim,
-           q_hbm, k_hbm, v_hbm, c_hbm, no_hbm, gq_hbm, gk_hbm, gv_hbm,
-           io, st0, st1, st2, st3, qh, kh, vh, ch, raw, gr,
+           q_hbm, k_hbm, v_hbm, c_hbm, no_ref, gq_ref, gk_ref, gv_ref,
+           io, st0, st1, qh, kh, vh, ch, raw, gvp, gr,
            own, rs, rp, rx, sp, sx, low, acc, ex_send, ex_recv,
-           in_sem, out_sem, rs_s, rs_r, rp_s, rp_r, rx_s, rx_r, ex_s, ex_r):
+           in_sem, rs_s, rs_r, rp_s, rp_r, rx_s, rx_r, ex_s, ex_r):
     half = heads // 2
     pairs = n // 2
     rows = toks * heads
     width = heads * nh * dim
-    stages = (st0, st1, st2, st3)
-    outs = (no_hbm, gq_hbm, gk_hbm, gv_hbm)
     seq = lax.axis_index("seq")
     me = lax.axis_index("head")
     pair = seq // 2
@@ -46,8 +44,10 @@
     own_base = side * half
     oth_base = (1 - side) * half
 
+    landing = (no_ref, gq_ref, io.at[0], io.at[1])
+    stages = (st0, st1, gk_ref, gv_ref)
     loads = [
-        pltpu.make_async_copy(src, io.at[a], in_sem.at[a])
+        pltpu.make_async_copy(src, landing[a], in_sem.at[a])
         for a, src in enumerate((k_hbm, v_hbm, q_hbm, c_hbm))
     ]
     for load in loads:
@@ -75,23 +75,16 @@
     def widen(a):
         def body(j, _):
             at = pl.ds(pl.multiple_of(j * chunk, chunk), chunk)
-            stages[a][at, :] = io[a, at, :].astype(F32)
+            stages[a][at, :] = landing[a][at, :].astype(F32)
             return 0
         lax.fori_loop(0, 16, body, 0)
 
-    def store_copy(a, j):
-        part = rows // PARTS
-        at = pl.ds(j * part, part)
-        return pltpu.make_async_copy(io.at[a, at], outs[a].at[at], out_sem.at[a, j])
-
-    def narrow(a):
-        for j in range(PARTS):
-            def body(t, _, j=j):
-                at = pl.ds(pl.multiple_of((j * (16 // PARTS) + t) * chunk, chunk), chunk)
-                io[a, at, :] = stages[a][at, :].astype(BF16)
-                return 0
-            lax.fori_loop(0, 16 // PARTS, body, 0)
-            store_copy(a, j).start()
+    def narrow(stage, out):
+        def body(j, _):
+            at = pl.ds(pl.multiple_of(j * chunk, chunk), chunk)
+            out[at, :] = stage[at, :].astype(BF16)
+            return 0
+        lax.fori_loop(0, 16, body, 0)
 
     def swap(ph, c):
         return pltpu.make_async_remote_copy(
@@ -141,37 +134,55 @@
         hand(ph, c).wait_recv()
         low[ph, oth_base + c] = rx[ph, c].astype(BF16)
 
-    def scan(ph, unit, finish, after_units):
+    def scan(ph, state, before, unit, finish, after):
         at = place(ph)
 
-        def done_units(c):
-            return jnp.where(c < 0, 0, jnp.minimum(heads, 2 * (c + 1) + 5 * at))
-
-        def done_takes(c):
+        def units_by(c):
+            lead = jnp.where(at == 0, 0, half * at // (2 * (pairs - 1)) + (c + 1) // 2)
+            return jnp.where(c < 0, 0, jnp.minimum(half, lead))
+
+        def others_by(c):
+            return jnp.where(at == 0, jnp.minimum(half, c + 4), half)
+
+        def owns_by(c):
+            return jnp.where(c < 0, 0, jnp.maximum(c + 1, units_by(c)))
+
+        def finished_by(c):
+            return jnp.where(c < 0, 0, jnp.minimum(c + 1, units_by(c)))
+
+        def takes_by(c):
             lag = 2 + 2 * (pairs - 1 - at)
-            return jnp.clip(c + 1 - lag, 0, half)
-
-        def slot(c, _):
-            def one(u, _):
-                unit(jnp.where(u % 2 == 0, own_base, oth_base) + u // 2)
+            return jnp.clip(c + 1 - lag, 0, units_by(c))
+
+        def run(low_end, high_end, step):
+            def body(c, _):
+                step(c)
                 return 0
-            lax.fori_loop(done_units(c - 1), done_units(c), one, 0)
-            if after_units is not None:
-                @pl.when((done_units(c) == heads) & (done_units(c - 1) < heads))
-                def _():
-                    after_units()
-            relay(ph, c)
-            finish(own_base + c)
-            lax.fori_loop(done_takes(c - 1), done_takes(c), take_one, 0)
-            return 0
-
-        def take_one(c, _):
+            lax.fori_loop(low_end, high_end, body, 0)
+
+        def other(c):
+            state(oth_base + c)
+            swap(ph, c).start()
+
+        def take_one(c):
             take(ph, c)
             finish(oth_base + c)
-            return 0
-
-        lax.fori_loop(0, half, slot, 0)
-        lax.fori_loop(done_takes(half - 1), half, take_one, 0)
+
+        def slot(c):
+            run(others_by(c - 1), others_by(c), other)
+            run(owns_by(c - 1), owns_by(c), lambda j: state(own_base + j))
+            run(units_by(c - 1), units_by(c), unit)
+            relay(ph, c)
+            run(finished_by(c - 1), finished_by(c), lambda j: finish(own_base + j))
+            run(takes_by(c - 1), takes_by(c), take_one)
+
+        run(0, others_by(-1), other)
+        before()
+        run(0, half, slot)
+        run(units_by(half - 1), half, unit)
+        run(finished_by(half - 1), half, lambda j: finish(own_base + j))
+        after()
+        run(takes_by(half - 1), half, take_one)
 
     for ph in range(2):
         @pl.when(place(ph) == 0)
@@ -193,28 +204,11 @@
         vh[h] = v
         own[0, h] = dot_tn(k, v)
 
-    def kv_other(c, _):
-        kv_state(oth_base + c)
-        swap(0, c).start()
-        return 0
-
-    def kv_own(c, _):
-        kv_state(own_base + c)
-        return 0
-
-    lax.fori_loop(0, half, kv_other, 0)
-    lax.fori_loop(0, half, kv_own, 0)
-    loads[2].wait()
-    widen(2)
-    loads[3].wait()
-    widen(3)
-
-    def split_qc(h, _):
-        qh[h] = strided(st2, h)[...].astype(BF16)
-        ch[h] = strided(st3, h)[...].astype(BF16)
-        return 0
-
-    lax.fori_loop(0, heads, split_qc, 0)
+    def rest_of_inputs():
+        loads[2].wait()
+        widen(2)
+        loads[3].wait()
+        widen(3)
 
     rest = toks - CUT
 
@@ -239,10 +233,14 @@
         w1 = keep(above((rest, rest)), dot_nt(a[CUT:], b[CUT:]))
         return dot(w0, c), dot(w1, c[CUT:])
 
-    def local_out(h):
-        first, second = lower(qh[h], kh[h], vh[h])
-        raw[h, :CUT] = first
-        raw[h, CUT:] = second
+    def local_out(j):
+        for h in (own_base + j, oth_base + j):
+            q = strided(gk_ref, h)[...].astype(BF16)
+            qh[h] = q
+            ch[h] = strided(gv_ref, h)[...].astype(BF16)
+            first, second = lower(q, kh[h], vh[h])
+            raw[h, :CUT] = first
+            raw[h, CUT:] = second
 
     def finish_out(h):
         r = raw[h] + dot(qh[h], low[0, h])
@@ -250,7 +248,7 @@
         acc[0] += r * r
         acc[1] += ch[h].astype(F32) * r
 
-    scan(0, local_out, finish_out, None)
+    scan(0, kv_state, rest_of_inputs, local_out, finish_out, lambda: None)
 
     sq = jnp.sum(acc[0].T, axis=0, keepdims=True)
     inner = jnp.sum(acc[1].T, axis=0, keepdims=True)
@@ -279,39 +277,28 @@
         gr[h] = g
         own[1, h] = dot_tn(qh[h], g)
 
-    def qg_other(c, _):
-        qg_state(oth_base + c)
-        swap(1, c).start()
-        return 0
-
-    def qg_own(c, _):
-        qg_state(own_base + c)
-        return 0
-
-    lax.fori_loop(0, half, qg_other, 0)
-    lax.fori_loop(0, half, qg_own, 0)
-
-    def local_grads(h):
-        q, k, v, g = qh[h], kh[h], vh[h], gr[h]
-        strided(st0, h)[...] = raw[h] * acc[0]
-        first, second = lower(g, v, k)
-        strided(st1, h)[...] = jnp.concatenate([first, second], axis=0) + dot_nt(g, low[0, h])
-        first, second = upper(v, g, q)
-        strided(st2, h)[...] = jnp.concatenate([first, second], axis=0)
-        first, second = upper(k, q, g)
-        strided(st3, h)[...] = jnp.concatenate([first, second], axis=0)
+    def local_grads(j):
+        for h in (own_base + j, oth_base + j):
+            q, k, v, g = qh[h], kh[h], vh[h], gr[h]
+            strided(st0, h)[...] = raw[h] * acc[0]
+            first, second = lower(g, v, k)
+            strided(st1, h)[...] = jnp.concatenate([first, second], axis=0) + dot_nt(g, low[0, h])
+            first, second = upper(v, g, q)
+            raw[h, :CUT] = first
+            raw[h, CUT:] = second
+            first, second = upper(k, q, g)
+            gvp[h, :CUT] = first
+            gvp[h, CUT:] = second
+
+    def finish_grads(h):
+        strided(gk_ref, h)[...] = raw[h] + dot_nt(vh[h], low[1, h])
+        strided(gv_ref, h)[...] = gvp[h] + dot(kh[h], low[1, h])
 
     def early_outs():
-        narrow(0)
-        narrow(1)
-
-    def finish_grads(h):
-        strided(st2, h)[...] = strided(st2, h)[...] + dot_nt(vh[h], low[1, h])
-        strided(st3, h)[...] = strided(st3, h)[...] + dot(kh[h], low[1, h])
-
-    scan(1, local_grads, finish_grads, early_outs)
-    narrow(2)
-    narrow(3)
+        narrow(st0, no_ref)
+        narrow(st1, gq_ref)
+
+    scan(1, qg_state, lambda: None, local_grads, finish_grads, early_outs)
 
     for peer in peers:
         peer.wait_send()
@@ -325,9 +312,31 @@
                 chain(ph, c).wait_send()
             return 0
         lax.fori_loop(0, half, drain, 0)
-    for a in range(4):
+
+
+def write_out(no_ref, gq_ref, gk_ref, gv_ref, no_hbm, gq_hbm, gk_hbm, gv_hbm, low, sem, part_sem):
+    rows = no_ref.shape[0]
+    part = rows // PARTS
+    copies = [
+        pltpu.make_async_copy(no_ref, no_hbm, sem.at[0]),
+        pltpu.make_async_copy(gq_ref, gq_hbm, sem.at[1]),
+    ]
+    for copy in copies:
+        copy.start()
+    chunk = part // 4
+    for a, (src, dst) in enumerate(((gk_ref, gk_hbm), (gv_ref, gv_hbm))):
         for j in range(PARTS):
-            store_copy(a, j).wait()
+            def body(t, _):
+                at = pl.ds(pl.multiple_of(j * part + t * chunk, chunk), chunk)
+                low[a, at, :] = src[at, :].astype(BF16)
+                return 0
+            lax.fori_loop(0, 4, body, 0)
+            at = pl.ds(j * part, part)
+            copy = pltpu.make_async_copy(low.at[a, at], dst.at[at], part_sem.at[a, j])
+            copy.start()
+            copies.append(copy)
+    for copy in copies:
+        copy.wait()
 
 
 def local(n, nh, queries, keys, values, cotangent):
@@ -339,16 +348,17 @@
     sems = pltpu.SemaphoreType.DMA
     per_head = pltpu.VMEM((heads, toks, dim), BF16)
     part = pltpu.VMEM((2, half, dim, dim), F32)
-    outs = pl.pallas_call(
+    in_vmem = pl.BlockSpec(memory_space=pltpu.VMEM)
+    made = pl.pallas_call(
         functools.partial(kernel, n, nh, heads, toks, dim),
-        out_shape=[jax.ShapeDtypeStruct((rows, dim), BF16)] * 4,
+        out_shape=[pltpu.VMEM((rows, dim), kind) for kind in (BF16, BF16, F32, F32)],
         in_specs=[any_spec] * 4,
-        out_specs=[any_spec] * 4,
+        out_specs=[in_vmem] * 4,
         scratch_shapes=[
-            pltpu.VMEM((4, rows, dim), BF16),
-            *[pltpu.VMEM((rows, dim), F32)] * 4,
+            pltpu.VMEM((2, rows, dim), BF16),
+            *[pltpu.VMEM((rows, dim), F32)] * 2,
             *[per_head] * 4,
-            pltpu.VMEM((heads, toks, dim), F32),
+            *[pltpu.VMEM((heads, toks, dim), F32)] * 2,
             per_head,
             pltpu.VMEM((2, heads, dim, dim), F32),
             *[part] * 5,
@@ -357,16 +367,24 @@
             pltpu.VMEM((8, toks), F32),
             pltpu.VMEM((nh - 1, 8, toks), F32),
             sems((4,)),
-            sems((4, PARTS)),
             *[sems((2, half))] * 6,
             sems((nh - 1,)),
             sems((nh - 1,)),
         ],
         compiler_params=pltpu.CompilerParams(
-            collective_id=0, has_side_effects=True, vmem_limit_bytes=60 * 2**20),
+            collective_id=0, has_side_effects=True, vmem_limit_bytes=44 * 2**20),
         cost_estimate=pl.CostEstimate(
-            flops=heads * 10 * toks * toks * dim, bytes_accessed=16 * rows * dim, transcendentals=toks),
+            flops=heads * 10 * toks * toks * dim, bytes_accessed=8 * rows * dim, transcendentals=toks),
     )(*flat)
+    outs = pl.pallas_call(
+        write_out,
+        out_shape=[jax.ShapeDtypeStruct((rows, dim), BF16)] * 4,
+        in_specs=[in_vmem] * 4,
+        out_specs=[any_spec] * 4,
+        scratch_shapes=[pltpu.VMEM((2, rows, dim), BF16), sems((2,)), sems((2, PARTS))],
+        compiler_params=pltpu.CompilerParams(vmem_limit_bytes=16 * 2**20),
+        cost_estimate=pl.CostEstimate(flops=0, bytes_accessed=8 * rows * dim, transcendentals=0),
+    )(*made)
     return tuple(x.reshape(toks, heads, dim) for x in outs)
 
 

time: 100 us -> 86 us (0.86)
  the two profiles are of different devices: /device:TPU:0 before, /device:TPU:24 now
where the time goes in v2:
time: 86 us; the launch traced here: 85.9 us
  Pallas kernels  85.2 us (99%)
    pallas_call x1, Pallas kernels, local(): pl.pallas_call(functools.partial(kernel, n, nh, heads, toks, dim), out_sh...  81.9 us
    pallas_call x1, Pallas kernels, local(): pl.pallas_call(write_out, out_shape=[jax.ShapeDtypeStruct((rows, dim), BF...  3.37 us

profile of v2, /device:TPU:24, one launch (start us, length us, event | category | flops | bytes accessed | tf_op | source)
XLA Modules:
  0.0 85.9 jit_solution(18040055238171965099)
XLA Ops:
  0.6 81.9 %shard_map.75 = (bf16[8192,128]{1,0:T(8,128)(2,1)S(1)}, bf16[8192,128]{1,0:T(8,128)(2,1)S(1)}, f32[8192,128]{1,0:T(8,128)S(1)}, f32[8192,128]{1,0:T(8,128)S(1)}) custom-call(bf16[8192,128]{1,0:T(8,128)(2,1)} %bitcast.8, bf16[8192,128]{1,0:T(8,128)(2,1)} %bitcast.9, bf16[8192,128]{1,0:T(8,128)(2,1)} %bitcast.10, bf16[8192,128]{1,0:T(8,128)(2,1)} %bitcast.11), custom_call_target="tpu_custom_call" | custom-call | flops 5368709120 | bytes 8388608 | tf_op jit(solution)/shard_map/pallas_call | solution.py:352
  82.5 3.4 %shard_map.76 = (bf16[8192,128]{1,0:T(8,128)(2,1)}, bf16[8192,128]{1,0:T(8,128)(2,1)}, bf16[8192,128]{1,0:T(8,128)(2,1)}, bf16[8192,128]{1,0:T(8,128)(2,1)}) custom-call(bf16[8192,128]{1,0:T(8,128)(2,1)S(1)} %get-tuple-element.12.no_ref, bf16[8192,128]{1,0:T(8,128)(2,1)S(1)} %get-tuple-element.13.gq_ref, f32[8192,128]{1,0:T(8,128)S(1)} %get-tuple-element.14.gk_ref, ...), custom_call_target="tpu_custom_call" | custom-call | bytes 8388608 | tf_op jit(solution)/shard_map/pallas_call | solution.py:379

commit v3 on v2

--- a/solution.py
+++ b/solution.py
@@ -10,6 +10,7 @@
 EPSILON = 1e-06
 CUT = 256
 PARTS = 4
+TOKS_STEP = 16
 F32 = jnp.float32
 BF16 = jnp.bfloat16
 MESH = pl.DeviceIdType.MESH
@@ -25,6 +26,39 @@
 
 def dot_tn(a, b):
     return lax.dot_general(a, b, (((0,), (0,)), ((), ())), preferred_element_type=F32)
+
+
+def token_rows(heads, token, group):
+    return pl.ds(group * 8 * (token[1] + 1) + token[0], 8, stride=token[1] + 1)
+
+
+def spread(src, dst, heads):
+    toks = src.shape[0] // heads
+
+    def body(j, _):
+        start = j * TOKS_STEP
+        x = src[pl.ds(pl.multiple_of(start * heads, TOKS_STEP * heads), TOKS_STEP * heads), :].astype(F32)
+        for t in range(TOKS_STEP):
+            for group in range(heads // 8):
+                at = t * heads + group * 8
+                dst[token_rows(heads, (start + t, toks), group), :] = x[at:at + 8]
+        return 0
+    lax.fori_loop(0, toks // TOKS_STEP, body, 0)
+
+
+def gather(src, dst, heads, first, count):
+    toks = dst.shape[0] // heads
+
+    def body(j, _):
+        start = first + j * TOKS_STEP
+        x = jnp.concatenate([
+            src[token_rows(heads, (start + t, toks), group), :]
+            for t in range(TOKS_STEP) for group in range(heads // 8)
+        ], axis=0)
+        at = pl.ds(pl.multiple_of(start * heads, TOKS_STEP * heads), TOKS_STEP * heads)
+        dst[at, :] = x.astype(BF16)
+        return 0
+    lax.fori_loop(0, count // TOKS_STEP, body, 0)
 
 
 def kernel(n, nh, heads, toks, dim,
@@ -67,24 +101,8 @@
     for d in range(1, nh):
         pl.semaphore_signal(barrier, inc=1, device_id={"head": (me + d) % nh}, device_id_type=MESH)
 
-    def strided(ref, h):
-        return ref.at[pl.ds(h, toks, stride=heads), :]
-
-    chunk = rows // 16
-
-    def widen(a):
-        def body(j, _):
-            at = pl.ds(pl.multiple_of(j * chunk, chunk), chunk)
-            stages[a][at, :] = landing[a][at, :].astype(F32)
-            return 0
-        lax.fori_loop(0, 16, body, 0)
-
-    def narrow(stage, out):
-        def body(j, _):
-            at = pl.ds(pl.multiple_of(j * chunk, chunk), chunk)
-            out[at, :] = stage[at, :].astype(BF16)
-            return 0
-        lax.fori_loop(0, 16, body, 0)
+    def of_head(ref, h):
+        return ref.at[pl.ds(h * (toks + 1), toks), :]
 
     def swap(ph, c):
         return pltpu.make_async_remote_copy(
@@ -138,11 +156,11 @@
         at = place(ph)
 
         def units_by(c):
-            lead = jnp.where(at == 0, 0, half * at // (2 * (pairs - 1)) + (c + 1) // 2)
+            lead = jnp.where(at == 0, (c + 1) // 3, half * at // (2 * (pairs - 1)) + (c + 1) // 2)
             return jnp.where(c < 0, 0, jnp.minimum(half, lead))
 
         def others_by(c):
-            return jnp.where(at == 0, jnp.minimum(half, c + 4), half)
+            return jnp.where(at == 0, jnp.clip(c + 4, 0, half), half)
 
         def owns_by(c):
             return jnp.where(c < 0, 0, jnp.maximum(c + 1, units_by(c)))
@@ -191,24 +209,24 @@
 
     acc[...] = jnp.zeros(acc.shape, F32)
     loads[0].wait()
-    widen(0)
+    spread(landing[0], stages[0], heads)
     loads[1].wait()
-    widen(1)
+    spread(landing[1], stages[1], heads)
     pl.semaphore_wait(
         barrier, nh + jnp.where(pair > 0, 1, 0) + jnp.where(pair < pairs - 1, 1, 0))
 
     def kv_state(h):
-        k = strided(st0, h)[...].astype(BF16)
-        v = strided(st1, h)[...].astype(BF16)
+        k = of_head(st0, h)[...].astype(BF16)
+        v = of_head(st1, h)[...].astype(BF16)
         kh[h] = k
         vh[h] = v
         own[0, h] = dot_tn(k, v)
 
     def rest_of_inputs():
         loads[2].wait()
-        widen(2)
+        spread(landing[2], stages[2], heads)
         loads[3].wait()
-        widen(3)
+        spread(landing[3], stages[3], heads)
 
     rest = toks - CUT
 
@@ -235,9 +253,9 @@
 
     def local_out(j):
         for h in (own_base + j, oth_base + j):
-            q = strided(gk_ref, h)[...].astype(BF16)
+            q = of_head(gk_ref, h)[...].astype(BF16)
             qh[h] = q
-            ch[h] = strided(gv_ref, h)[...].astype(BF16)
+            ch[h] = of_head(gv_ref, h)[...].astype(BF16)
             first, second = lower(q, kh[h], vh[h])
             raw[h, :CUT] = first
             raw[h, CUT:] = second
@@ -280,9 +298,9 @@
     def local_grads(j):
         for h in (own_base + j, oth_base + j):
             q, k, v, g = qh[h], kh[h], vh[h], gr[h]
-            strided(st0, h)[...] = raw[h] * acc[0]
+            of_head(st0, h)[...] = raw[h] * acc[0]
             first, second = lower(g, v, k)
-            strided(st1, h)[...] = jnp.concatenate([first, second], axis=0) + dot_nt(g, low[0, h])
+            of_head(st1, h)[...] = jnp.concatenate([first, second], axis=0) + dot_nt(g, low[0, h])
             first, second = upper(v, g, q)
             raw[h, :CUT] = first
             raw[h, CUT:] = second
@@ -291,12 +309,12 @@
             gvp[h, CUT:] = second
 
     def finish_grads(h):
-        strided(gk_ref, h)[...] = raw[h] + dot_nt(vh[h], low[1, h])
-        strided(gv_ref, h)[...] = gvp[h] + dot(kh[h], low[1, h])
+        of_head(gk_ref, h)[...] = raw[h] + dot_nt(vh[h], low[1, h])
+        of_head(gv_ref, h)[...] = gvp[h] + dot(kh[h], low[1, h])
 
     def early_outs():
-        narrow(st0, no_ref)
-        narrow(st1, gq_ref)
+        gather(st0, no_ref, heads, 0, toks)
+        gather(st1, gq_ref, heads, 0, toks)
 
     scan(1, qg_state, lambda: None, local_grads, finish_grads, early_outs)
 
@@ -314,25 +332,22 @@
         lax.fori_loop(0, half, drain, 0)
 
 
-def write_out(no_ref, gq_ref, gk_ref, gv_ref, no_hbm, gq_hbm, gk_hbm, gv_hbm, low, sem, part_sem):
+def write_out(heads, no_ref, gq_ref, gk_ref, gv_ref, no_hbm, gq_hbm, gk_hbm, gv_hbm,
+              low_k, low_v, sem, part_sem):
     rows = no_ref.shape[0]
     part = rows // PARTS
+    toks = rows // heads
     copies = [
         pltpu.make_async_copy(no_ref, no_hbm, sem.at[0]),
         pltpu.make_async_copy(gq_ref, gq_hbm, sem.at[1]),
     ]
     for copy in copies:
         copy.start()
-    chunk = part // 4
-    for a, (src, dst) in enumerate(((gk_ref, gk_hbm), (gv_ref, gv_hbm))):
+    for a, (src, low, dst) in enumerate(((gk_ref, low_k, gk_hbm), (gv_ref, low_v, gv_hbm))):
         for j in range(PARTS):
-            def body(t, _):
-                at = pl.ds(pl.multiple_of(j * part + t * chunk, chunk), chunk)
-                low[a, at, :] = src[at, :].astype(BF16)
-                return 0
-            lax.fori_loop(0, 4, body, 0)
+            gather(src, low, heads, j * (toks // PARTS), toks // PARTS)
             at = pl.ds(j * part, part)
-            copy = pltpu.make_async_copy(low.at[a, at], dst.at[at], part_sem.at[a, j])
+            copy = pltpu.make_async_copy(low.at[at], dst.at[at], part_sem.at[a, j])
             copy.start()
             copies.append(copy)
     for copy in copies:
@@ -351,12 +366,12 @@
     in_vmem = pl.BlockSpec(memory_space=pltpu.VMEM)
     made = pl.pallas_call(
         functools.partial(kernel, n, nh, heads, toks, dim),
-        out_shape=[pltpu.VMEM((rows, dim), kind) for kind in (BF16, BF16, F32, F32)],
+        out_shape=[pltpu.VMEM((rows, dim), BF16)] * 2 + [pltpu.VMEM((rows + heads, dim), F32)] * 2,
         in_specs=[any_spec] * 4,
         out_specs=[in_vmem] * 4,
         scratch_shapes=[
             pltpu.VMEM((2, rows, dim), BF16),
-            *[pltpu.VMEM((rows, dim), F32)] * 2,
+            *[pltpu.VMEM((rows + heads, dim), F32)] * 2,
             *[per_head] * 4,
             *[pltpu.VMEM((heads, toks, dim), F32)] * 2,
             per_head,
@@ -377,11 +392,11 @@
             flops=heads * 10 * toks * toks * dim, bytes_accessed=8 * rows * dim, transcendentals=toks),
     )(*flat)
     outs = pl.pallas_call(
-        write_out,
+        functools.partial(write_out, heads),
         out_shape=[jax.ShapeDtypeStruct((rows, dim), BF16)] * 4,
         in_specs=[in_vmem] * 4,
         out_specs=[any_spec] * 4,
-        scratch_shapes=[pltpu.VMEM((2, rows, dim), BF16), sems((2,)), sems((2, PARTS))],
+        scratch_shapes=[*[pltpu.VMEM((rows, dim), BF16)] * 2, sems((2,)), sems((2, PARTS))],
         compiler_params=pltpu.CompilerParams(vmem_limit_bytes=16 * 2**20),
         cost_estimate=pl.CostEstimate(flops=0, bytes_accessed=8 * rows * dim, transcendentals=0),
     )(*made)

time: 86 us -> 79.1 us (0.920)
  the two profiles are of different devices: /device:TPU:24 before, /device:TPU:0 now
where the time goes in v3:
time: 79.1 us; the launch traced here: 79 us
  Pallas kernels  78.3 us (99%)
    pallas_call x1, Pallas kernels, local(): pl.pallas_call(functools.partial(kernel, n, nh, heads, toks, dim), out_sh...  75 us
    pallas_call x1, Pallas kernels, local(): pl.pallas_call(functools.partial(write_out, heads), out_shape=[jax.ShapeD...  3.37 us

profile of v3, /device:TPU:0, one launch (start us, length us, event | category | flops | bytes accessed | tf_op | source)
XLA Modules:
  0.0 79.0 jit_solution(10088195967804645500)
XLA Ops:
  0.6 75.0 %shard_map.75 = (bf16[8192,128]{1,0:T(8,128)(2,1)S(1)}, bf16[8192,128]{1,0:T(8,128)(2,1)S(1)}, f32[8208,128]{1,0:T(8,128)S(1)}, f32[8208,128]{1,0:T(8,128)S(1)}) custom-call(bf16[8192,128]{1,0:T(8,128)(2,1)} %bitcast.8, bf16[8192,128]{1,0:T(8,128)(2,1)} %bitcast.9, bf16[8192,128]{1,0:T(8,128)(2,1)} %bitcast.10, bf16[8192,128]{1,0:T(8,128)(2,1)} %bitcast.11), custom_call_target="tpu_custom_call" | custom-call | flops 5368709120 | bytes 8388608 | tf_op jit(solution)/shard_map/pallas_call | solution.py:367
  75.6 3.4 %shard_map.76 = (bf16[8192,128]{1,0:T(8,128)(2,1)}, bf16[8192,128]{1,0:T(8,128)(2,1)}, bf16[8192,128]{1,0:T(8,128)(2,1)}, bf16[8192,128]{1,0:T(8,128)(2,1)}) custom-call(bf16[8192,128]{1,0:T(8,128)(2,1)S(1)} %get-tuple-element.12.no_ref, bf16[8192,128]{1,0:T(8,128)(2,1)S(1)} %get-tuple-element.13.gq_ref, f32[8208,128]{1,0:T(8,128)S(1)} %get-tuple-element.14.gk_ref, ...), custom_call_target="tpu_custom_call" | custom-call | bytes 8388608 | tf_op jit(solution)/shard_map/pallas_call | solution.py:394

commit v4 on v3

--- a/solution.py
+++ b/solution.py
@@ -84,8 +84,8 @@
         pltpu.make_async_copy(src, landing[a], in_sem.at[a])
         for a, src in enumerate((k_hbm, v_hbm, q_hbm, c_hbm))
     ]
-    for load in loads:
-        load.start()
+    loads[0].start()
+    loads[1].start()
 
     barrier = pltpu.get_barrier_semaphore()
     pl.semaphore_signal(barrier, inc=1, device_id={"seq": partner}, device_id_type=MESH)
@@ -145,7 +145,6 @@
             chain(ph, c).start()
 
         sx[ph, c] = so_far + jnp.where(later, 0.0, mine)
-        hand(ph, c).start()
         low[ph, own_base + c] = (so_far + jnp.where(later, theirs, 0.0)).astype(BF16)
 
     def take(ph, c):
@@ -156,7 +155,8 @@
         at = place(ph)
 
         def units_by(c):
-            lead = jnp.where(at == 0, (c + 1) // 3, half * at // (2 * (pairs - 1)) + (c + 1) // 2)
+            lead = half * at // (2 * (pairs - 1)) + (c + 1) * at // (pairs - 1)
+            lead = jnp.where(at == 0, (c + 1) // 3, lead)
             return jnp.where(c < 0, 0, jnp.minimum(half, lead))
 
         def others_by(c):
@@ -168,9 +168,13 @@
         def finished_by(c):
             return jnp.where(c < 0, 0, jnp.minimum(c + 1, units_by(c)))
 
+        defer = half * (pairs - 1 - at) // (pairs - 1)
+
+        def hands_by(c):
+            return jnp.clip(c + 1 - defer, 0, half)
+
         def takes_by(c):
-            lag = 2 + 2 * (pairs - 1 - at)
-            return jnp.clip(c + 1 - lag, 0, units_by(c))
+            return jnp.clip(c - 1 - defer, 0, units_by(c))
 
         def run(low_end, high_end, step):
             def body(c, _):
@@ -182,6 +186,9 @@
             state(oth_base + c)
             swap(ph, c).start()
 
+        def give(c):
+            hand(ph, c).start()
+
         def take_one(c):
             take(ph, c)
             finish(oth_base + c)
@@ -190,16 +197,25 @@
             run(others_by(c - 1), others_by(c), other)
             run(owns_by(c - 1), owns_by(c), lambda j: state(own_base + j))
             run(units_by(c - 1), units_by(c), unit)
+            if after is not None:
+                @pl.when((units_by(c) == half) & (units_by(c - 1) < half))
+                def _():
+                    after()
             relay(ph, c)
+            run(hands_by(c - 1), hands_by(c), give)
             run(finished_by(c - 1), finished_by(c), lambda j: finish(own_base + j))
             run(takes_by(c - 1), takes_by(c), take_one)
 
         run(0, others_by(-1), other)
         before()
         run(0, half, slot)
+        run(hands_by(half - 1), half, give)
         run(units_by(half - 1), half, unit)
+        if after is not None:
+            @pl.when(units_by(half - 1) < half)
+            def _():
+                after()
         run(finished_by(half - 1), half, lambda j: finish(own_base + j))
-        after()
         run(takes_by(half - 1), half, take_one)
 
     for ph in range(2):
@@ -209,6 +225,8 @@
 
     acc[...] = jnp.zeros(acc.shape, F32)
     loads[0].wait()
+    loads[2].start()
+    loads[3].start()
     spread(landing[0], stages[0], heads)
     loads[1].wait()
     spread(landing[1], stages[1], heads)
@@ -228,27 +246,25 @@
         loads[3].wait()
         spread(landing[3], stages[3], heads)
 
-    rest = toks - CUT
-
-    def below(shape, shift):
-        return (lax.broadcasted_iota(jnp.int32, shape, 1)
-                <= lax.broadcasted_iota(jnp.int32, shape, 0) + shift)
-
-    def above(shape):
-        return (lax.broadcasted_iota(jnp.int32, shape, 1)
-                >= lax.broadcasted_iota(jnp.int32, shape, 0))
+    def square(compare):
+        return compare(lax.broadcasted_iota(jnp.int32, (CUT, CUT), 1),
+                       lax.broadcasted_iota(jnp.int32, (CUT, CUT), 0))
 
     def keep(mask, x):
         return jnp.where(mask, x, 0.0).astype(BF16)
 
     def lower(a, b, c):
-        w0 = keep(below((CUT, CUT), 0), dot_nt(a[:CUT], b[:CUT]))
-        w1 = keep(below((rest, toks), CUT), dot_nt(a[CUT:], b))
+        mask = square(jnp.less_equal)
+        w0 = keep(mask, dot_nt(a[:CUT], b[:CUT]))
+        w1 = dot_nt(a[CUT:], b)
+        w1 = jnp.concatenate([w1[:, :CUT].astype(BF16), keep(mask, w1[:, CUT:])], axis=1)
         return dot(w0, c[:CUT]), dot(w1, c)
 
     def upper(a, b, c):
-        w0 = keep(above((CUT, toks)), dot_nt(a[:CUT], b))
-        w1 = keep(above((rest, rest)), dot_nt(a[CUT:], b[CUT:]))
+        mask = square(jnp.greater_equal)
+        w0 = dot_nt(a[:CUT], b)
+        w0 = jnp.concatenate([keep(mask, w0[:, :CUT]), w0[:, CUT:].astype(BF16)], axis=1)
+        w1 = keep(mask, dot_nt(a[CUT:], b[CUT:]))
         return dot(w0, c), dot(w1, c[CUT:])
 
     def local_out(j):
@@ -266,7 +282,7 @@
         acc[0] += r * r
         acc[1] += ch[h].astype(F32) * r
 
-    scan(0, kv_state, rest_of_inputs, local_out, finish_out, lambda: None)
+    scan(0, kv_state, rest_of_inputs, local_out, finish_out, None)
 
     sq = jnp.sum(acc[0].T, axis=0, keepdims=True)
     inner = jnp.sum(acc[1].T, axis=0, keepdims=True)

time: 79.1 us -> 73.1 us (0.924)
  Pallas kernels: 78.3 us -> 72.3 us
    pallas_call x1, Pallas kernels: 75 us -> 69 us  [local(): pl.pallas_call(functools.partial(kernel, n, nh, heads, toks, dim), out_sh...]
where the time goes in v4:
time: 73.1 us; the launch traced here: 73 us
  Pallas kernels  72.3 us (99%)
    pallas_call x1, Pallas kernels, local(): pl.pallas_call(functools.partial(kernel, n, nh, heads, toks, dim), out_sh...  69 us
    pallas_call x1, Pallas kernels, local(): pl.pallas_call(functools.partial(write_out, heads), out_shape=[jax.ShapeD...  3.37 us

profile of v4, /device:TPU:0, one launch (start us, length us, event | category | flops | bytes accessed | tf_op | source)
XLA Modules:
  0.0 73.0 jit_solution(14199394636306110579)
XLA Ops:
  0.6 69.0 %shard_map.75 = (bf16[8192,128]{1,0:T(8,128)(2,1)S(1)}, bf16[8192,128]{1,0:T(8,128)(2,1)S(1)}, f32[8208,128]{1,0:T(8,128)S(1)}, f32[8208,128]{1,0:T(8,128)S(1)}) custom-call(bf16[8192,128]{1,0:T(8,128)(2,1)} %bitcast.8, bf16[8192,128]{1,0:T(8,128)(2,1)} %bitcast.9, bf16[8192,128]{1,0:T(8,128)(2,1)} %bitcast.10, bf16[8192,128]{1,0:T(8,128)(2,1)} %bitcast.11), custom_call_target="tpu_custom_call" | custom-call | flops 5368709120 | bytes 8388608 | tf_op jit(solution)/shard_map/pallas_call | solution.py:383
  69.6 3.4 %shard_map.76 = (bf16[8192,128]{1,0:T(8,128)(2,1)}, bf16[8192,128]{1,0:T(8,128)(2,1)}, bf16[8192,128]{1,0:T(8,128)(2,1)}, bf16[8192,128]{1,0:T(8,128)(2,1)}) custom-call(bf16[8192,128]{1,0:T(8,128)(2,1)S(1)} %get-tuple-element.12.no_ref, bf16[8192,128]{1,0:T(8,128)(2,1)S(1)} %get-tuple-element.13.gq_ref, f32[8208,128]{1,0:T(8,128)S(1)} %get-tuple-element.14.gk_ref, ...), custom_call_target="tpu_custom_call" | custom-call | bytes 8388608 | tf_op jit(solution)/shard_map/pallas_call | solution.py:410

commit v5 on v4

--- a/solution.py
+++ b/solution.py
@@ -10,6 +10,7 @@
 EPSILON = 1e-06
 CUT = 256
 PARTS = 4
+PIECES = 2
 TOKS_STEP = 16
 F32 = jnp.float32
 BF16 = jnp.bfloat16
@@ -32,14 +33,14 @@
     return pl.ds(group * 8 * (token[1] + 1) + token[0], 8, stride=token[1] + 1)
 
 
-def spread(src, dst, heads):
+def spread(src, dst, heads, groups):
     toks = src.shape[0] // heads
 
     def body(j, _):
         start = j * TOKS_STEP
         x = src[pl.ds(pl.multiple_of(start * heads, TOKS_STEP * heads), TOKS_STEP * heads), :].astype(F32)
         for t in range(TOKS_STEP):
-            for group in range(heads // 8):
+            for group in groups:
                 at = t * heads + group * 8
                 dst[token_rows(heads, (start + t, toks), group), :] = x[at:at + 8]
         return 0
@@ -110,11 +111,11 @@
             send_sem=rs_s.at[ph, c], recv_sem=rs_r.at[ph, c],
             device_id={"seq": partner}, device_id_type=MESH)
 
-    def chain(ph, c):
+    def chain(ph, c, piece):
         nxt = (seq + 2) % n if ph == 0 else (seq + n - 2) % n
         return pltpu.make_async_remote_copy(
-            src_ref=sp.at[ph, c], dst_ref=rp.at[ph, c],
-            send_sem=rp_s.at[ph, c], recv_sem=rp_r.at[ph, c],
+            src_ref=sp.at[ph, c, rows_of(piece)], dst_ref=rp.at[ph, c, rows_of(piece)],
+            send_sem=rp_s.at[ph, c, piece], recv_sem=rp_r.at[ph, c, piece],
             device_id={"seq": nxt}, device_id_type=MESH)
 
     def hand(ph, c):
@@ -126,37 +127,41 @@
     def place(ph):
         return pair if ph == 0 else pairs - 1 - pair
 
+    def rows_of(piece):
+        return pl.ds(piece * (dim // PIECES), dim // PIECES)
+
     def relay(ph, c):
         at = place(ph)
         later = (side == 1) if ph == 0 else (side == 0)
         swap(ph, c).wait_recv()
-        mine = own[ph, own_base + c]
-        theirs = rs[ph, c]
-
-        @pl.when(at > 0)
-        def _():
-            chain(ph, c).wait_recv()
-
-        so_far = rp[ph, c]
-
-        @pl.when(at < pairs - 1)
-        def _():
-            sp[ph, c] = so_far + (mine + theirs)
-            chain(ph, c).start()
-
-        sx[ph, c] = so_far + jnp.where(later, 0.0, mine)
-        low[ph, own_base + c] = (so_far + jnp.where(later, theirs, 0.0)).astype(BF16)
+        for piece in range(PIECES):
+            some = rows_of(piece)
+            mine = own[ph, own_base + c, some, :]
+            theirs = rs[ph, c, some, :]
+
+            @pl.when(at > 0)
+            def _():
+                chain(ph, c, piece).wait_recv()
+
+            so_far = rp[ph, c, some, :]
+
+            @pl.when(at < pairs - 1)
+            def _():
+                sp[ph, c, some, :] = so_far + (mine + theirs)
+                chain(ph, c, piece).start()
+
+            sx[ph, c, some, :] = so_far + jnp.where(later, 0.0, mine)
+            low[ph, own_base + c, some, :] = (so_far + jnp.where(later, theirs, 0.0)).astype(BF16)
 
     def take(ph, c):
         hand(ph, c).wait_recv()
         low[ph, oth_base + c] = rx[ph, c].astype(BF16)
 
-    def scan(ph, state, before, unit, finish, after):
+    def scan(ph, state, ahead, before, unit, finish, after):
         at = place(ph)
 
         def units_by(c):
             lead = half * at // (2 * (pairs - 1)) + (c + 1) * at // (pairs - 1)
-            lead = jnp.where(at == 0, (c + 1) // 3, lead)
             return jnp.where(c < 0, 0, jnp.minimum(half, lead))
 
         def others_by(c):
@@ -207,9 +212,14 @@
             run(takes_by(c - 1), takes_by(c), take_one)
 
         run(0, others_by(-1), other)
-        before()
+        if ahead is not None:
+            ahead()
+        if before is not None:
+            pl.when(at > 0)(before)
         run(0, half, slot)
         run(hands_by(half - 1), half, give)
+        if before is not None:
+            pl.when(at == 0)(before)
         run(units_by(half - 1), half, unit)
         if after is not None:
             @pl.when(units_by(half - 1) < half)
@@ -227,9 +237,22 @@
     loads[0].wait()
     loads[2].start()
     loads[3].start()
-    spread(landing[0], stages[0], heads)
+    all_groups = range(heads // 8)
+    by_half = half % 8 == 0
+
+    def spread_half(a, which):
+        def of(groups):
+            spread(landing[a], stages[a], heads, groups)
+
+        if by_half:
+            pl.when(which == 0)(lambda: of(range(half // 8)))
+            pl.when(which == 1)(lambda: of(range(half // 8, heads // 8)))
+        else:
+            of(all_groups)
+
+    spread_half(0, 1 - side)
     loads[1].wait()
-    spread(landing[1], stages[1], heads)
+    spread_half(1, 1 - side)
     pl.semaphore_wait(
         barrier, nh + jnp.where(pair > 0, 1, 0) + jnp.where(pair < pairs - 1, 1, 0))
 
@@ -240,11 +263,16 @@
         vh[h] = v
         own[0, h] = dot_tn(k, v)
 
+    def rest_of_keys():
+        if by_half:
+            spread_half(0, side)
+            spread_half(1, side)
+
     def rest_of_inputs():
         loads[2].wait()
-        spread(landing[2], stages[2], heads)
+        spread(landing[2], stages[2], heads, all_groups)
         loads[3].wait()
-        spread(landing[3], stages[3], heads)
+        spread(landing[3], stages[3], heads, all_groups)
 
     def square(compare):
         return compare(lax.broadcasted_iota(jnp.int32, (CUT, CUT), 1),
@@ -282,7 +310,7 @@
         acc[0] += r * r
         acc[1] += ch[h].astype(F32) * r
 
-    scan(0, kv_state, rest_of_inputs, local_out, finish_out, None)
+    scan(0, kv_state, rest_of_keys, rest_of_inputs, local_out, finish_out, None)
 
     sq = jnp.sum(acc[0].T, axis=0, keepdims=True)
     inner = jnp.sum(acc[1].T, axis=0, keepdims=True)
@@ -332,7 +360,7 @@
         gather(st0, no_ref, heads, 0, toks)
         gather(st1, gq_ref, heads, 0, toks)
 
-    scan(1, qg_state, lambda: None, local_grads, finish_grads, early_outs)
+    scan(1, qg_state, None, None, local_grads, finish_grads, early_outs)
 
     for peer in peers:
         peer.wait_send()
@@ -343,7 +371,8 @@
 
             @pl.when(place(ph) < pairs - 1)
             def _():
-                chain(ph, c).wait_send()
+                for piece in range(PIECES):
+                    chain(ph, c, piece).wait_send()
             return 0
         lax.fori_loop(0, half, drain, 0)
 
@@ -398,7 +427,9 @@
             pltpu.VMEM((8, toks), F32),
             pltpu.VMEM((nh - 1, 8, toks), F32),
             sems((4,)),
-            *[sems((2, half))] * 6,
+            *[sems((2, half))] * 2,
+            *[sems((2, half, PIECES))] * 2,
+            *[sems((2, half))] * 2,
             sems((nh - 1,)),
             sems((nh - 1,)),
         ],

time: 73.1 us -> 72.4 us (level)
  no operation moved by 1% of the time
where the time goes in v5:
time: 72.4 us; the launch traced here: 72.2 us
  Pallas kernels  71.6 us (99%)
    pallas_call x1, Pallas kernels, local(): pl.pallas_call(functools.partial(kernel, n, nh, heads, toks, dim), out_sh...  68.2 us
    pallas_call x1, Pallas kernels, local(): pl.pallas_call(functools.partial(write_out, heads), out_shape=[jax.ShapeD...  3.37 us

profile of v5, /device:TPU:0, one launch (start us, length us, event | category | flops | bytes accessed | tf_op | source)
XLA Modules:
  0.0 72.2 jit_solution(5145547824733053685)
XLA Ops:
  0.6 68.2 %shard_map.75 = (bf16[8192,128]{1,0:T(8,128)(2,1)S(1)}, bf16[8192,128]{1,0:T(8,128)(2,1)S(1)}, f32[8208,128]{1,0:T(8,128)S(1)}, f32[8208,128]{1,0:T(8,128)S(1)}) custom-call(bf16[8192,128]{1,0:T(8,128)(2,1)} %bitcast.8, bf16[8192,128]{1,0:T(8,128)(2,1)} %bitcast.9, bf16[8192,128]{1,0:T(8,128)(2,1)} %bitcast.10, bf16[8192,128]{1,0:T(8,128)(2,1)} %bitcast.11), custom_call_target="tpu_custom_call" | custom-call | flops 5368709120 | bytes 8388608 | tf_op jit(solution)/shard_map/pallas_call | solution.py:412
  68.9 3.4 %shard_map.76 = (bf16[8192,128]{1,0:T(8,128)(2,1)}, bf16[8192,128]{1,0:T(8,128)(2,1)}, bf16[8192,128]{1,0:T(8,128)(2,1)}, bf16[8192,128]{1,0:T(8,128)(2,1)}) custom-call(bf16[8192,128]{1,0:T(8,128)(2,1)S(1)} %get-tuple-element.12.no_ref, bf16[8192,128]{1,0:T(8,128)(2,1)S(1)} %get-tuple-element.13.gq_ref, f32[8208,128]{1,0:T(8,128)S(1)} %get-tuple-element.14.gk_ref, ...), custom_call_target="tpu_custom_call" | custom-call | bytes 8388608 | tf_op jit(solution)/shard_map/pallas_call | solution.py:441

commit v6 on v5

--- a/solution.py
+++ b/solution.py
@@ -157,21 +157,14 @@
         hand(ph, c).wait_recv()
         low[ph, oth_base + c] = rx[ph, c].astype(BF16)
 
+    batch = 4 if half % 4 == 0 else 1
+
     def scan(ph, state, ahead, before, unit, finish, after):
         at = place(ph)
 
         def units_by(c):
             lead = half * at // (2 * (pairs - 1)) + (c + 1) * at // (pairs - 1)
             return jnp.where(c < 0, 0, jnp.minimum(half, lead))
-
-        def others_by(c):
-            return jnp.where(at == 0, jnp.clip(c + 4, 0, half), half)
-
-        def owns_by(c):
-            return jnp.where(c < 0, 0, jnp.maximum(c + 1, units_by(c)))
-
-        def finished_by(c):
-            return jnp.where(c < 0, 0, jnp.minimum(c + 1, units_by(c)))
 
         defer = half * (pairs - 1 - at) // (pairs - 1)
 
@@ -187,20 +180,22 @@
                 return 0
             lax.fori_loop(low_end, high_end, body, 0)
 
-        def other(c):
-            state(oth_base + c)
-            swap(ph, c).start()
-
         def give(c):
             hand(ph, c).start()
 
+        def others(j):
+            state([oth_base + j * batch + i for i in range(batch)])
+            for i in range(batch):
+                swap(ph, j * batch + i).start()
+
+        def owns(j):
+            state([own_base + j * batch + i for i in range(batch)])
+
         def take_one(c):
             take(ph, c)
-            finish(oth_base + c)
+            finish([own_base + c, oth_base + c])
 
         def slot(c):
-            run(others_by(c - 1), others_by(c), other)
-            run(owns_by(c - 1), owns_by(c), lambda j: state(own_base + j))
             run(units_by(c - 1), units_by(c), unit)
             if after is not None:
                 @pl.when((units_by(c) == half) & (units_by(c - 1) < half))
@@ -208,12 +203,12 @@
                     after()
             relay(ph, c)
             run(hands_by(c - 1), hands_by(c), give)
-            run(finished_by(c - 1), finished_by(c), lambda j: finish(own_base + j))
             run(takes_by(c - 1), takes_by(c), take_one)
 
-        run(0, others_by(-1), other)
+        run(0, half // batch, others)
         if ahead is not None:
             ahead()
+        run(0, half // batch, owns)
         if before is not None:
             pl.when(at > 0)(before)
         run(0, half, slot)
@@ -225,7 +220,6 @@
             @pl.when(units_by(half - 1) < half)
             def _():
                 after()
-        run(finished_by(half - 1), half, lambda j: finish(own_base + j))
         run(takes_by(half - 1), half, take_one)
 
     for ph in range(2):
@@ -256,12 +250,13 @@
     pl.semaphore_wait(
         barrier, nh + jnp.where(pair > 0, 1, 0) + jnp.where(pair < pairs - 1, 1, 0))
 
-    def kv_state(h):
-        k = of_head(st0, h)[...].astype(BF16)
-        v = of_head(st1, h)[...].astype(BF16)
-        kh[h] = k
-        vh[h] = v
-        own[0, h] = dot_tn(k, v)
+    def kv_state(at_once):
+        for h in at_once:
+            k = of_head(st0, h)[...].astype(BF16)
+            v = of_head(st1, h)[...].astype(BF16)
+            kh[h] = k
+            vh[h] = v
+            own[0, h] = dot_tn(k, v)
 
     def rest_of_keys():
         if by_half:
@@ -304,11 +299,18 @@
             raw[h, :CUT] = first
             raw[h, CUT:] = second
 
-    def finish_out(h):
-        r = raw[h] + dot(qh[h], low[0, h])
-        raw[h] = r
-        acc[0] += r * r
-        acc[1] += ch[h].astype(F32) * r
+    blocks = [pl.ds(start, CUT // 2) for start in range(0, toks, CUT // 2)]
+
+    def finish_out(at_once):
+        for some in blocks:
+            squares, products = acc[0, some, :], acc[1, some, :]
+            for h in at_once:
+                r = raw[h, some, :] + dot(qh[h, some, :], low[0, h])
+                raw[h, some, :] = r
+                squares += r * r
+                products += ch[h, some, :].astype(F32) * r
+            acc[0, some, :] = squares
+            acc[1, some, :] = products
 
     scan(0, kv_state, rest_of_keys, rest_of_inputs, local_out, finish_out, None)
 
@@ -334,10 +336,12 @@
     acc[0] = jnp.broadcast_to(inv, (dim, toks)).T
     acc[1] = jnp.broadcast_to(inv * slope, (dim, toks)).T
 
-    def qg_state(h):
-        g = (acc[0] * (ch[h].astype(F32) - raw[h] * acc[1])).astype(BF16)
-        gr[h] = g
-        own[1, h] = dot_tn(qh[h], g)
+    def qg_state(at_once):
+        for h in at_once:
+            for some in blocks:
+                gr[h, some, :] = (acc[0, some, :] * (
+                    ch[h, some, :].astype(F32) - raw[h, some, :] * acc[1, some, :])).astype(BF16)
+            own[1, h] = dot_tn(qh[h], gr[h])
 
     def local_grads(j):
         for h in (own_base + j, oth_base + j):
@@ -352,9 +356,10 @@
             gvp[h, :CUT] = first
             gvp[h, CUT:] = second
 
-    def finish_grads(h):
-        of_head(gk_ref, h)[...] = raw[h] + dot_nt(vh[h], low[1, h])
-        of_head(gv_ref, h)[...] = gvp[h] + dot(kh[h], low[1, h])
+    def finish_grads(at_once):
+        for h in at_once:
+            of_head(gk_ref, h)[...] = raw[h] + dot_nt(vh[h], low[1, h])
+            of_head(gv_ref, h)[...] = gvp[h] + dot(kh[h], low[1, h])
 
     def early_outs():
         gather(st0, no_ref, heads, 0, toks)

time: 72.4 us -> 72.2 us (level)
  no operation moved by 1% of the time
where the time goes in v6:
time: 72.2 us; the launch traced here: 72 us
  Pallas kernels  71.4 us (99%)
    pallas_call x1, Pallas kernels, local(): pl.pallas_call(functools.partial(kernel, n, nh, heads, toks, dim), out_sh...  68 us
    pallas_call x1, Pallas kernels, local(): pl.pallas_call(functools.partial(write_out, heads), out_shape=[jax.ShapeD...  3.37 us

profile of v6, /device:TPU:0, one launch (start us, length us, event | category | flops | bytes accessed | tf_op | source)
XLA Modules:
  0.0 72.0 jit_solution(10203938936157804753)
XLA Ops:
  0.6 68.0 %shard_map.75 = (bf16[8192,128]{1,0:T(8,128)(2,1)S(1)}, bf16[8192,128]{1,0:T(8,128)(2,1)S(1)}, f32[8208,128]{1,0:T(8,128)S(1)}, f32[8208,128]{1,0:T(8,128)S(1)}) custom-call(bf16[8192,128]{1,0:T(8,128)(2,1)} %bitcast.8, bf16[8192,128]{1,0:T(8,128)(2,1)} %bitcast.9, bf16[8192,128]{1,0:T(8,128)(2,1)} %bitcast.10, bf16[8192,128]{1,0:T(8,128)(2,1)} %bitcast.11), custom_call_target="tpu_custom_call" | custom-call | flops 5368709120 | bytes 8388608 | tf_op jit(solution)/shard_map/pallas_call | solution.py:417
  68.7 3.4 %shard_map.76 = (bf16[8192,128]{1,0:T(8,128)(2,1)}, bf16[8192,128]{1,0:T(8,128)(2,1)}, bf16[8192,128]{1,0:T(8,128)(2,1)}, bf16[8192,128]{1,0:T(8,128)(2,1)}) custom-call(bf16[8192,128]{1,0:T(8,128)(2,1)S(1)} %get-tuple-element.12.no_ref, bf16[8192,128]{1,0:T(8,128)(2,1)S(1)} %get-tuple-element.13.gq_ref, f32[8208,128]{1,0:T(8,128)S(1)} %get-tuple-element.14.gk_ref, ...), custom_call_target="tpu_custom_call" | custom-call | bytes 8388608 | tf_op jit(solution)/shard_map/pallas_call | solution.py:446

commit v7 on v6

--- a/solution.py
+++ b/solution.py
@@ -163,10 +163,10 @@
         at = place(ph)
 
         def units_by(c):
-            lead = half * at // (2 * (pairs - 1)) + (c + 1) * at // (pairs - 1)
+            lead = half * at // (2 * (pairs - 1)) + (c + 1) // 2
             return jnp.where(c < 0, 0, jnp.minimum(half, lead))
 
-        defer = half * (pairs - 1 - at) // (pairs - 1)
+        defer = jnp.maximum(0, half * (pairs - 1 - at) // (pairs - 1) - half // 4)
 
         def hands_by(c):
             return jnp.clip(c + 1 - defer, 0, half)
@@ -184,9 +184,9 @@
             hand(ph, c).start()
 
         def others(j):
-            state([oth_base + j * batch + i for i in range(batch)])
-            for i in range(batch):
-                swap(ph, j * batch + i).start()
+            state([oth_base + j * 2 + i for i in range(2)])
+            for i in range(2):
+                swap(ph, j * 2 + i).start()
 
         def owns(j):
             state([own_base + j * batch + i for i in range(batch)])
@@ -197,29 +197,21 @@
 
         def slot(c):
             run(units_by(c - 1), units_by(c), unit)
-            if after is not None:
-                @pl.when((units_by(c) == half) & (units_by(c - 1) < half))
-                def _():
-                    after()
             relay(ph, c)
             run(hands_by(c - 1), hands_by(c), give)
             run(takes_by(c - 1), takes_by(c), take_one)
 
-        run(0, half // batch, others)
+        run(0, half // 2, others)
         if ahead is not None:
             ahead()
         run(0, half // batch, owns)
         if before is not None:
-            pl.when(at > 0)(before)
+            before()
         run(0, half, slot)
         run(hands_by(half - 1), half, give)
-        if before is not None:
-            pl.when(at == 0)(before)
         run(units_by(half - 1), half, unit)
         if after is not None:
-            @pl.when(units_by(half - 1) < half)
-            def _():
-                after()
+            after()
         run(takes_by(half - 1), half, take_one)
 
     for ph in range(2):

time: 72.2 us -> 74.8 us (1.036)
  Pallas kernels: 71.4 us -> 74 us
    pallas_call x1, Pallas kernels: 68 us -> 70.7 us  [local(): pl.pallas_call(functools.partial(kernel, n, nh, heads, toks, dim), out_sh...]
where the time goes in v7:
time: 74.8 us; the launch traced here: 74.7 us
  Pallas kernels  74 us (99%)
    pallas_call x1, Pallas kernels, local(): pl.pallas_call(functools.partial(kernel, n, nh, heads, toks, dim), out_sh...  70.7 us
    pallas_call x1, Pallas kernels, local(): pl.pallas_call(functools.partial(write_out, heads), out_shape=[jax.ShapeD...  3.37 us

profile of v7, /device:TPU:0, one launch (start us, length us, event | category | flops | bytes accessed | tf_op | source)
XLA Modules:
  0.0 74.7 jit_solution(12739316799232248810)
XLA Ops:
  0.6 70.7 %shard_map.75 = (bf16[8192,128]{1,0:T(8,128)(2,1)S(1)}, bf16[8192,128]{1,0:T(8,128)(2,1)S(1)}, f32[8208,128]{1,0:T(8,128)S(1)}, f32[8208,128]{1,0:T(8,128)S(1)}) custom-call(bf16[8192,128]{1,0:T(8,128)(2,1)} %bitcast.8, bf16[8192,128]{1,0:T(8,128)(2,1)} %bitcast.9, bf16[8192,128]{1,0:T(8,128)(2,1)} %bitcast.10, bf16[8192,128]{1,0:T(8,128)(2,1)} %bitcast.11), custom_call_target="tpu_custom_call" | custom-call | flops 5368709120 | bytes 8388608 | tf_op jit(solution)/shard_map/pallas_call | solution.py:409
  71.3 3.4 %shard_map.76 = (bf16[8192,128]{1,0:T(8,128)(2,1)}, bf16[8192,128]{1,0:T(8,128)(2,1)}, bf16[8192,128]{1,0:T(8,128)(2,1)}, bf16[8192,128]{1,0:T(8,128)(2,1)}) custom-call(bf16[8192,128]{1,0:T(8,128)(2,1)S(1)} %get-tuple-element.12.no_ref, bf16[8192,128]{1,0:T(8,128)(2,1)S(1)} %get-tuple-element.13.gq_ref, f32[8208,128]{1,0:T(8,128)S(1)} %get-tuple-element.14.gk_ref, ...), custom_call_target="tpu_custom_call" | custom-call | bytes 8388608 | tf_op jit(solution)/shard_map/pallas_call | solution.py:438
